TPU v7x, 128 devices: a whole 4x4x4 slice. The times are simulated.
128 devices in a mesh: fam: 4 (over z), ctx: 32 (over x, y, core).
Axes of the slice: x: 4, y: 4, z: 4, core: 2. Of those that a mesh axis runs over, the one named last changes fastest.
Arguments:
- queries: bfloat16 [4, 16384, 1024], P('fam', 'ctx'), may hold values from -7 to 7
- key_rows: bfloat16 [4, 16384, 1024], P('fam', 'ctx'), may hold values from -4 to 4
- value_rows: bfloat16 [4, 16384, 1024], P('fam', 'ctx'), may hold values from -6 to 6
- cotangent: bfloat16 [4, 16384, 1024], P('fam', 'ctx'), may hold values from -6 to 6
- out_weight: bfloat16 [1024, 1024], replicated, may hold values from -0.1875 to 0.1875
- prot_blocks: int32 [4, 32], P('fam'), may hold values from 1 to 8, 128 in all within a row
- last_fill: int32 [4, 32], P('fam'), may hold values from 1 to 128
- memory_slots: int32 [4, 512], P('fam'), may hold values from 0 to 511
Outputs:
- query_grad: bfloat16 [4, 16384, 1024], P('fam', 'ctx')
- key_grad: bfloat16 [4, 16384, 1024], P('fam', 'ctx')
- value_grad: bfloat16 [4, 16384, 1024], P('fam', 'ctx')
- weight_grad: float32 [1024, 1024], replicated
Inputs may be any that keep to these rules, and one draw needn't show every extreme that they name: `prot_blocks`: each family's protein lengths, in blocks, sum to 128, and the longest has exactly 8 blocks.
All inputs are finite; a program needn't handle non-finite values.
Results may differ from a plain program's by a relative error of at most 0.015.
Values may be sent and summed in bfloat16 or wider, within the bound.
A program may use at most 128 MiB of HBM per device.

v0:
```python
import jax
import jax.numpy as jnp
from jax import lax
from jax.sharding import PartitionSpec as P

HEAD_DIM = 64
W = 512
BLK = 128
NEG_FILL = -1e30


def passed_along(value, axis, steps):
    count = lax.axis_size(axis)
    initial, last = (max(0, -steps), min(count, count - steps))
    return lax.ppermute(value, axis, [(source, source + steps) for source in range(initial, last)])


def protein_tables(prot_blocks, last_fill):
    prot_ends = jnp.cumsum(prot_blocks)
    starts = prot_ends - prot_blocks
    valid_len = (prot_blocks - 1) * BLK + last_fill
    return (prot_ends, starts, valid_len)


def token_info(positions, tables):
    prot_ends, starts, valid_len = tables
    prot_count = prot_ends.shape[0]
    block_ids = jnp.floor_divide(positions, BLK)
    protein = jnp.sum((block_ids[:, None] >= prot_ends[None, :]).astype(jnp.int32), axis=1)
    onehot = protein[:, None] == jnp.arange(prot_count, dtype=jnp.int32)[None, :]
    first_block = jnp.sum(jnp.where(onehot, starts[None, :], 0), axis=1)
    allowed = jnp.sum(jnp.where(onehot, valid_len[None, :], 0), axis=1)
    is_valid = (positions >= 0) & (protein < prot_count) & (positions - first_block * BLK < allowed)
    return (protein, is_valid)


def band_mask(query_pos, query_info, key_pos, key_info):
    return (
        query_info[1][:, None]
        & key_info[1][None, :]
        & (query_info[0][:, None] == key_info[0][None, :])
        & (key_pos[None, :] <= query_pos[:, None])
        & (query_pos[:, None] - key_pos[None, :] < W)
    )


def columns_of(array, column, span):
    return lax.dynamic_slice_in_dim(array, column, span, 1)


def add_into(target, update, row_start, column):
    row_index = jnp.asarray(row_start, jnp.int32)
    current = lax.dynamic_slice(target, (row_index, column), update.shape)
    return lax.dynamic_update_slice(target, current + update, (row_index, column))


def attend(query_blk, grad_blk, key_blk, value_blk, live_mask):
    scale = HEAD_DIM ** (-0.5)
    scores = (
        jnp.einsum("qge,kge->gqk", query_blk, key_blk, preferred_element_type=jnp.float32) * scale
    )
    live = live_mask[None]
    shifted = jnp.where(live, scores, NEG_FILL)
    row_max = jnp.max(shifted, axis=-1, keepdims=True)
    expo = jnp.where(live, jnp.exp(shifted - row_max), 0.0)
    row_sum = jnp.maximum(jnp.sum(expo, axis=-1, keepdims=True), 1.0)
    attn_prob = expo / row_sum
    prob_half = attn_prob.astype(jnp.bfloat16)
    attended = jnp.einsum(
        "gqk,kge->qge", prob_half, value_blk, preferred_element_type=jnp.float32
    ).astype(jnp.bfloat16)
    grad_prob = jnp.einsum("qge,kge->gqk", grad_blk, value_blk, preferred_element_type=jnp.float32)
    row_dot = jnp.sum(attn_prob * grad_prob, axis=-1, keepdims=True)
    grad_score = (attn_prob * (grad_prob - row_dot) * scale).astype(jnp.bfloat16)
    grad_query = jnp.einsum("gqk,kge->qge", grad_score, key_blk, preferred_element_type=jnp.float32)
    grad_key = jnp.einsum("gqk,qge->kge", grad_score, query_blk, preferred_element_type=jnp.float32)
    grad_value = jnp.einsum("gqk,qge->kge", prob_half, grad_blk, preferred_element_type=jnp.float32)
    return (attended, grad_query, grad_key, grad_value, row_max, row_sum, row_dot)


def per_device(
    queries, key_rows, value_rows, cotangent, out_weight, prot_blocks, last_fill, memory_slots
):
    query_loc = queries[0]
    key_loc = key_rows[0]
    value_loc = value_rows[0]
    grad_out = cotangent[0]
    tables = protein_tables(prot_blocks[0], last_fill[0])
    slots = memory_slots[0]
    tokens, width = query_loc.shape
    span = 2 * HEAD_DIM
    pair_count = width // span
    heads_total = width // HEAD_DIM
    ctx_size = lax.axis_size("ctx")
    ctx_index = lax.axis_index("ctx")
    slot_total = slots.shape[0]
    slot_dev = slot_total // ctx_size
    base = ctx_index * tokens
    positions = base + jnp.arange(tokens, dtype=jnp.int32)
    own_info = token_info(positions, tables)
    ext_pos = base - W + jnp.arange(W + tokens, dtype=jnp.int32)
    ext_info = token_info(ext_pos, tables)
    source = jnp.arange(slot_total, dtype=jnp.int32) // slot_dev * tokens + slots
    mem_info = token_info(source, tables)
    own_slots = lax.dynamic_slice_in_dim(slots, ctx_index * slot_dev, slot_dev)
    mem_keys, mem_values = (
        lax.all_gather(key_loc[own_slots], "ctx", axis=0, tiled=True),
        lax.all_gather(value_loc[own_slots], "ctx", axis=0, tiled=True),
    )
    halo_keys, halo_values = passed_along((key_loc, value_loc), "ctx", 1)
    ext_keys = jnp.concatenate([halo_keys, key_loc], axis=0)
    ext_values = jnp.concatenate([halo_values, value_loc], axis=0)
    grad_attn = jnp.einsum(
        "te,de->td", grad_out, out_weight, preferred_element_type=jnp.float32
    ).astype(jnp.bfloat16)
    masks = []
    query_info = (own_info[0], own_info[1])
    key_info = (ext_info[0], ext_info[1])
    band = band_mask(positions, query_info, ext_pos, key_info)
    memory = (
        query_info[1][:, None]
        & mem_info[1][None, :]
        & (mem_info[0][None, :] < query_info[0][:, None])
    )
    masks.append(jnp.concatenate([band, memory], axis=1))

    def pair_step(head_pair, carry):
        (
            query_grad,
            band_kgrad,
            band_vgrad,
            mem_kgrad,
            mem_vgrad,
            attn_rows,
            stat_max,
            stat_sum,
            stat_dot,
        ) = carry
        column = head_pair * span
        query_pair = columns_of(query_loc, column, span).reshape(tokens, 2, HEAD_DIM)
        dout_pair = columns_of(grad_attn, column, span).reshape(tokens, 2, HEAD_DIM)
        key_band = columns_of(ext_keys, column, span).reshape(W + tokens, 2, HEAD_DIM)
        value_band = columns_of(ext_values, column, span).reshape(W + tokens, 2, HEAD_DIM)
        key_memory = columns_of(mem_keys, column, span).reshape(slot_total, 2, HEAD_DIM)
        value_memory = columns_of(mem_values, column, span).reshape(slot_total, 2, HEAD_DIM)
        key_blk = jnp.concatenate([key_band, key_memory], axis=0)
        value_blk = jnp.concatenate([value_band, value_memory], axis=0)
        attended, grad_query, grad_key, grad_value, row_max, row_sum, row_dot = attend(
            query_pair, dout_pair, key_blk, value_blk, masks[0]
        )
        row_index = jnp.asarray(0, jnp.int32)
        query_grad = lax.dynamic_update_slice(
            query_grad, grad_query.reshape(W, span), (row_index, column)
        )
        attn_rows = lax.dynamic_update_slice(
            attn_rows, attended.reshape(W, span), (row_index, column)
        )
        band_kgrad = add_into(band_kgrad, grad_key[: 2 * W].reshape(2 * W, span), 0, column)
        band_vgrad = add_into(band_vgrad, grad_value[: 2 * W].reshape(2 * W, span), 0, column)
        mem_kgrad = add_into(mem_kgrad, grad_key[2 * W :].reshape(slot_total, span), 0, column)
        mem_vgrad = add_into(mem_vgrad, grad_value[2 * W :].reshape(slot_total, span), 0, column)
        stat_col = head_pair * 2
        zero_row = jnp.asarray(0, jnp.int32)
        stat_max = lax.dynamic_update_slice(stat_max, row_max[:, :, 0].T, (zero_row, stat_col))
        stat_sum = lax.dynamic_update_slice(stat_sum, row_sum[:, :, 0].T, (zero_row, stat_col))
        stat_dot = lax.dynamic_update_slice(stat_dot, row_dot[:, :, 0].T, (zero_row, stat_col))
        return (
            query_grad,
            band_kgrad,
            band_vgrad,
            mem_kgrad,
            mem_vgrad,
            attn_rows,
            stat_max,
            stat_sum,
            stat_dot,
        )

    init = (
        jnp.zeros((tokens, width), jnp.float32),
        jnp.zeros((W + tokens, width), jnp.float32),
        jnp.zeros((W + tokens, width), jnp.float32),
        jnp.zeros((slot_total, width), jnp.float32),
        jnp.zeros((slot_total, width), jnp.float32),
        jnp.zeros((tokens, width), jnp.bfloat16),
        jnp.zeros((W, heads_total), jnp.float32),
        jnp.zeros((W, heads_total), jnp.float32),
        jnp.zeros((W, heads_total), jnp.float32),
    )
    (
        query_grad,
        band_kgrad,
        band_vgrad,
        mem_kgrad,
        mem_vgrad,
        attn_rows,
        stat_max,
        stat_sum,
        stat_dot,
    ) = lax.fori_loop(0, pair_count, pair_step, init)
    own_kgrad = band_kgrad[W:]
    own_vgrad = band_vgrad[W:]
    back_kgrad, back_vgrad = (
        passed_along(band_kgrad[:W].astype(jnp.bfloat16), "ctx", -1).astype(jnp.float32),
        passed_along(band_vgrad[:W].astype(jnp.bfloat16), "ctx", -1).astype(jnp.float32),
    )
    own_kgrad = own_kgrad.at[tokens - W :].add(back_kgrad)
    own_vgrad = own_vgrad.at[tokens - W :].add(back_vgrad)
    got_kgrad, got_vgrad = (
        lax.psum_scatter(
            mem_kgrad.astype(jnp.bfloat16), "ctx", scatter_dimension=0, tiled=True
        ).astype(jnp.float32),
        lax.psum_scatter(
            mem_vgrad.astype(jnp.bfloat16), "ctx", scatter_dimension=0, tiled=True
        ).astype(jnp.float32),
    )
    own_kgrad = own_kgrad.at[own_slots].add(got_kgrad)
    own_vgrad = own_vgrad.at[own_slots].add(got_vgrad)
    weight_part = lax.dot_general(
        attn_rows, grad_out, (((0,), (0,)), ((), ())), preferred_element_type=jnp.float32
    )
    weight_total = lax.psum(weight_part, ("fam", "ctx"))
    weight_grad = weight_total * (lax.axis_size("fam") * ctx_size * tokens) ** (-0.5)
    return (
        query_grad.astype(jnp.bfloat16)[None],
        own_kgrad.astype(jnp.bfloat16)[None],
        own_vgrad.astype(jnp.bfloat16)[None],
        weight_grad,
    )


def solution(mesh):
    return jax.shard_map(
        per_device,
        mesh=mesh,
        in_specs=(
            P("fam", "ctx", None),
            P("fam", "ctx", None),
            P("fam", "ctx", None),
            P("fam", "ctx", None),
            P(),
            P("fam", None),
            P("fam", None),
            P("fam", None),
        ),
        out_specs=(P("fam", "ctx", None), P("fam", "ctx", None), P("fam", "ctx", None), P()),
        check_vma=False,
    )
```

profile of v0, /device:TPU:1, one launch (start us, length us, event | category | flops | bytes accessed | tf_op | source)
XLA Modules:
  0.0 967.8 jit_solution(17995845950725439622)
XLA Ops:
  44.0 19.9 %all-gather.7.cloned.1.call-done = bf16[512,1024]{1,0:T(8,128)(2,1)} async-done(((bf16[16,1024]{1,0:T(8,128)(2,1)}), bf16[512,1024]{1,0:T(8,128)(2,1)}) %all-gather.7.cloned.1.call-update) | async-done | bytes 1048592 | tf_op jit(solution)/shard_map/all_gather | solution.py:108
  63.9 44.9 %all-gather.5.cloned.1.call-done = bf16[512,1024]{1,0:T(8,128)(2,1)} async-done(((bf16[16,1024]{1,0:T(8,128)(2,1)}), bf16[512,1024]{1,0:T(8,128)(2,1)}) %all-gather.5.cloned.1.call-update) | async-done | bytes 1048592 | tf_op jit(solution)/shard_map/all_gather | solution.py:107
  118.0 518.4 %while.27 = (s32[]{:T(128)}, bf16[512,1024]{1,0:T(8,128)(2,1)}, f32[1024,1024]{1,0:T(8,128)}, f32[1024,1024]{1,0:T(8,128)}, f32[512,1024]{1,0:T(8,128)}, /*index...) while((s32[]{:T(128)}, bf16[512,1024]{1,0:T(8,128)(2,1)}, ...), condition=%wide.region_14.15_spmd, body=%wide.region_10.14_spmd.sunk | while | flops 1247747584 | bytes 80244984 | solution.py:200
  144.4 13.6 %fusion.101 = bf16[2,64,512]{2,1,0:T(8,128)(2,1)S(1)} fusion(f32[2,512,1536]{2,1,0:T(8,128)} %fusion.99, bf16[512,2,64]{0,2,1:T(8,128)(2,1)S(1)} %bitcast.109, bf16[1024,2,64]{0,2,1:T(8,128)(2,1)S(1)} %bitcast.104, f32[2,512,1536]{2,1,0:T(8,128)} %get-tuple-element.467, f32[2,512]{1,0:T(2,128)S(1)} %broadcast_maximum_fusion.2), kind=kOutput, calls=%fused_computation.16.clone.1 | convolution fusion | flops 213125632 | bytes 13111296 | tf_op jit(solution)/shard_map/while/body/eval_jaxpr/gqk,kge->qge/dot_general | solution.py:75
  157.9 13.2 %fusion.102 = f32[1536,2,64]{0,2,1:T(8,128)S(1)} fusion(bf16[512,2,64]{0,2,1:T(8,128)(2,1)S(1)} %bitcast.107, f32[2,512,1536]{2,1,0:T(8,128)} %fusion.99, f32[2,512,1536]{2,1,0:T(8,128)} %get-tuple-element.467, f32[2,512]{1,0:T(2,128)S(1)} %broadcast_maximum_fusion.2), kind=kOutput, calls=%fused_computation.18.clone.1 | convolution fusion | flops 212339200 | bytes 13504512 | tf_op jit(solution)/shard_map/while/body/eval_jaxpr/gqk,qge->kge/dot_general | solution.py:76
  209.2 13.6 %fusion.101 = bf16[2,64,512]{2,1,0:T(8,128)(2,1)S(1)} fusion(f32[2,512,1536]{2,1,0:T(8,128)} %fusion.99, bf16[512,2,64]{0,2,1:T(8,128)(2,1)S(1)} %bitcast.109, bf16[1024,2,64]{0,2,1:T(8,128)(2,1)S(1)} %bitcast.104, f32[2,512,1536]{2,1,0:T(8,128)} %get-tuple-element.467, f32[2,512]{1,0:T(2,128)S(1)} %broadcast_maximum_fusion.2), kind=kOutput, calls=%fused_computation.16.clone.1 | convolution fusion | flops 213125632 | bytes 13111296 | tf_op jit(solution)/shard_map/while/body/eval_jaxpr/gqk,kge->qge/dot_general | solution.py:75
  222.7 13.2 %fusion.102 = f32[1536,2,64]{0,2,1:T(8,128)S(1)} fusion(bf16[512,2,64]{0,2,1:T(8,128)(2,1)S(1)} %bitcast.107, f32[2,512,1536]{2,1,0:T(8,128)} %fusion.99, f32[2,512,1536]{2,1,0:T(8,128)} %get-tuple-element.467, f32[2,512]{1,0:T(2,128)S(1)} %broadcast_maximum_fusion.2), kind=kOutput, calls=%fused_computation.18.clone.1 | convolution fusion | flops 212339200 | bytes 13504512 | tf_op jit(solution)/shard_map/while/body/eval_jaxpr/gqk,qge->kge/dot_general | solution.py:76
  274.0 13.6 %fusion.101 = bf16[2,64,512]{2,1,0:T(8,128)(2,1)S(1)} fusion(f32[2,512,1536]{2,1,0:T(8,128)} %fusion.99, bf16[512,2,64]{0,2,1:T(8,128)(2,1)S(1)} %bitcast.109, bf16[1024,2,64]{0,2,1:T(8,128)(2,1)S(1)} %bitcast.104, f32[2,512,1536]{2,1,0:T(8,128)} %get-tuple-element.467, f32[2,512]{1,0:T(2,128)S(1)} %broadcast_maximum_fusion.2), kind=kOutput, calls=%fused_computation.16.clone.1 | convolution fusion | flops 213125632 | bytes 13111296 | tf_op jit(solution)/shard_map/while/body/eval_jaxpr/gqk,kge->qge/dot_general | solution.py:75
  287.5 13.2 %fusion.102 = f32[1536,2,64]{0,2,1:T(8,128)S(1)} fusion(bf16[512,2,64]{0,2,1:T(8,128)(2,1)S(1)} %bitcast.107, f32[2,512,1536]{2,1,0:T(8,128)} %fusion.99, f32[2,512,1536]{2,1,0:T(8,128)} %get-tuple-element.467, f32[2,512]{1,0:T(2,128)S(1)} %broadcast_maximum_fusion.2), kind=kOutput, calls=%fused_computation.18.clone.1 | convolution fusion | flops 212339200 | bytes 13504512 | tf_op jit(solution)/shard_map/while/body/eval_jaxpr/gqk,qge->kge/dot_general | solution.py:76
  338.8 13.6 %fusion.101 = bf16[2,64,512]{2,1,0:T(8,128)(2,1)S(1)} fusion(f32[2,512,1536]{2,1,0:T(8,128)} %fusion.99, bf16[512,2,64]{0,2,1:T(8,128)(2,1)S(1)} %bitcast.109, bf16[1024,2,64]{0,2,1:T(8,128)(2,1)S(1)} %bitcast.104, f32[2,512,1536]{2,1,0:T(8,128)} %get-tuple-element.467, f32[2,512]{1,0:T(2,128)S(1)} %broadcast_maximum_fusion.2), kind=kOutput, calls=%fused_computation.16.clone.1 | convolution fusion | flops 213125632 | bytes 13111296 | tf_op jit(solution)/shard_map/while/body/eval_jaxpr/gqk,kge->qge/dot_general | solution.py:75
  352.4 13.2 %fusion.102 = f32[1536,2,64]{0,2,1:T(8,128)S(1)} fusion(bf16[512,2,64]{0,2,1:T(8,128)(2,1)S(1)} %bitcast.107, f32[2,512,1536]{2,1,0:T(8,128)} %fusion.99, f32[2,512,1536]{2,1,0:T(8,128)} %get-tuple-element.467, f32[2,512]{1,0:T(2,128)S(1)} %broadcast_maximum_fusion.2), kind=kOutput, calls=%fused_computation.18.clone.1 | convolution fusion | flops 212339200 | bytes 13504512 | tf_op jit(solution)/shard_map/while/body/eval_jaxpr/gqk,qge->kge/dot_general | solution.py:76
  403.6 13.6 %fusion.101 = bf16[2,64,512]{2,1,0:T(8,128)(2,1)S(1)} fusion(f32[2,512,1536]{2,1,0:T(8,128)} %fusion.99, bf16[512,2,64]{0,2,1:T(8,128)(2,1)S(1)} %bitcast.109, bf16[1024,2,64]{0,2,1:T(8,128)(2,1)S(1)} %bitcast.104, f32[2,512,1536]{2,1,0:T(8,128)} %get-tuple-element.467, f32[2,512]{1,0:T(2,128)S(1)} %broadcast_maximum_fusion.2), kind=kOutput, calls=%fused_computation.16.clone.1 | convolution fusion | flops 213125632 | bytes 13111296 | tf_op jit(solution)/shard_map/while/body/eval_jaxpr/gqk,kge->qge/dot_general | solution.py:75
  417.2 13.2 %fusion.102 = f32[1536,2,64]{0,2,1:T(8,128)S(1)} fusion(bf16[512,2,64]{0,2,1:T(8,128)(2,1)S(1)} %bitcast.107, f32[2,512,1536]{2,1,0:T(8,128)} %fusion.99, f32[2,512,1536]{2,1,0:T(8,128)} %get-tuple-element.467, f32[2,512]{1,0:T(2,128)S(1)} %broadcast_maximum_fusion.2), kind=kOutput, calls=%fused_computation.18.clone.1 | convolution fusion | flops 212339200 | bytes 13504512 | tf_op jit(solution)/shard_map/while/body/eval_jaxpr/gqk,qge->kge/dot_general | solution.py:76
  468.4 13.6 %fusion.101 = bf16[2,64,512]{2,1,0:T(8,128)(2,1)S(1)} fusion(f32[2,512,1536]{2,1,0:T(8,128)} %fusion.99, bf16[512,2,64]{0,2,1:T(8,128)(2,1)S(1)} %bitcast.109, bf16[1024,2,64]{0,2,1:T(8,128)(2,1)S(1)} %bitcast.104, f32[2,512,1536]{2,1,0:T(8,128)} %get-tuple-element.467, f32[2,512]{1,0:T(2,128)S(1)} %broadcast_maximum_fusion.2), kind=kOutput, calls=%fused_computation.16.clone.1 | convolution fusion | flops 213125632 | bytes 13111296 | tf_op jit(solution)/shard_map/while/body/eval_jaxpr/gqk,kge->qge/dot_general | solution.py:75
  482.0 13.2 %fusion.102 = f32[1536,2,64]{0,2,1:T(8,128)S(1)} fusion(bf16[512,2,64]{0,2,1:T(8,128)(2,1)S(1)} %bitcast.107, f32[2,512,1536]{2,1,0:T(8,128)} %fusion.99, f32[2,512,1536]{2,1,0:T(8,128)} %get-tuple-element.467, f32[2,512]{1,0:T(2,128)S(1)} %broadcast_maximum_fusion.2), kind=kOutput, calls=%fused_computation.18.clone.1 | convolution fusion | flops 212339200 | bytes 13504512 | tf_op jit(solution)/shard_map/while/body/eval_jaxpr/gqk,qge->kge/dot_general | solution.py:76
  521.6 7.0 fusion.100
  533.2 13.6 %fusion.101 = bf16[2,64,512]{2,1,0:T(8,128)(2,1)S(1)} fusion(f32[2,512,1536]{2,1,0:T(8,128)} %fusion.99, bf16[512,2,64]{0,2,1:T(8,128)(2,1)S(1)} %bitcast.109, bf16[1024,2,64]{0,2,1:T(8,128)(2,1)S(1)} %bitcast.104, f32[2,512,1536]{2,1,0:T(8,128)} %get-tuple-element.467, f32[2,512]{1,0:T(2,128)S(1)} %broadcast_maximum_fusion.2), kind=kOutput, calls=%fused_computation.16.clone.1 | convolution fusion | flops 213125632 | bytes 13111296 | tf_op jit(solution)/shard_map/while/body/eval_jaxpr/gqk,kge->qge/dot_general | solution.py:75
  546.8 13.2 %fusion.102 = f32[1536,2,64]{0,2,1:T(8,128)S(1)} fusion(bf16[512,2,64]{0,2,1:T(8,128)(2,1)S(1)} %bitcast.107, f32[2,512,1536]{2,1,0:T(8,128)} %fusion.99, f32[2,512,1536]{2,1,0:T(8,128)} %get-tuple-element.467, f32[2,512]{1,0:T(2,128)S(1)} %broadcast_maximum_fusion.2), kind=kOutput, calls=%fused_computation.18.clone.1 | convolution fusion | flops 212339200 | bytes 13504512 | tf_op jit(solution)/shard_map/while/body/eval_jaxpr/gqk,qge->kge/dot_general | solution.py:76
  598.0 13.6 %fusion.101 = bf16[2,64,512]{2,1,0:T(8,128)(2,1)S(1)} fusion(f32[2,512,1536]{2,1,0:T(8,128)} %fusion.99, bf16[512,2,64]{0,2,1:T(8,128)(2,1)S(1)} %bitcast.109, bf16[1024,2,64]{0,2,1:T(8,128)(2,1)S(1)} %bitcast.104, f32[2,512,1536]{2,1,0:T(8,128)} %get-tuple-element.467, f32[2,512]{1,0:T(2,128)S(1)} %broadcast_maximum_fusion.2), kind=kOutput, calls=%fused_computation.16.clone.1 | convolution fusion | flops 213125632 | bytes 13111296 | tf_op jit(solution)/shard_map/while/body/eval_jaxpr/gqk,kge->qge/dot_general | solution.py:75
  611.6 13.2 %fusion.102 = f32[1536,2,64]{0,2,1:T(8,128)S(1)} fusion(bf16[512,2,64]{0,2,1:T(8,128)(2,1)S(1)} %bitcast.107, f32[2,512,1536]{2,1,0:T(8,128)} %fusion.99, f32[2,512,1536]{2,1,0:T(8,128)} %get-tuple-element.467, f32[2,512]{1,0:T(2,128)S(1)} %broadcast_maximum_fusion.2), kind=kOutput, calls=%fused_computation.18.clone.1 | convolution fusion | flops 212339200 | bytes 13504512 | tf_op jit(solution)/shard_map/while/body/eval_jaxpr/gqk,qge->kge/dot_general | solution.py:76
  660.6 9.2 collective-permute-done.2
  671.4 43.8 %reduce-scatter.5.cloned.1.call-done = bf16[16,1024]{1,0:T(8,128)(2,1)} async-done(((bf16[512,1024]{1,0:T(8,128)(2,1)}), bf16[16,1024]{1,0:T(8,128)(2,1)}) %reduce-scatter.5.cloned.1.call-update) | async-done | bytes 32784 | tf_op jit(solution)/shard_map/reduce_scatter | solution.py:213
  716.9 79.4 %reduce-scatter.3.cloned.1.call-done = bf16[16,1024]{1,0:T(8,128)(2,1)} async-done(((bf16[512,1024]{1,0:T(8,128)(2,1)}), bf16[16,1024]{1,0:T(8,128)(2,1)}) %reduce-scatter.3.cloned.1.call-update) | async-done | bytes 32784 | tf_op jit(solution)/shard_map/reduce_scatter | solution.py:210
  804.2 152.1 %all-reduce.2.cloned.1.call-done = f32[1024,1024]{1,0:T(8,128)} async-done(((f32[1024,1024]{1,0:T(8,128)}), f32[1024,1024]{1,0:T(8,128)}) %all-reduce.2.cloned.1.call-update) | async-done | bytes 4194320 | tf_op jit(solution)/shard_map/psum | solution.py:222
  (403 shorter events, 382.4 us)
Async XLA Ops:
  7.2 22.5 %copy-start = (bf16[1024,1024]{1,0:T(8,128)(2,1)S(1)}, bf16[1024,1024]{1,0:T(8,128)(2,1)}, u32[]{:S(2)}) copy-start(bf16[1024,1024]{1,0:T(8,128)(2,1)} %param.22) | copy-start | bytes 6291460
  7.2 56.7 %all-gather.7.cloned.1.call-start = ((), (), s32[]{:S(2)}) async-start(), calls=%async_computation.6 | async-start | bytes 1081344 | tf_op jit(solution)/shard_map/all_gather | solution.py:108
  8.1 0.5 copy-start.6
  11.2 97.5 %all-gather.5.cloned.1.call-start = ((), (), s32[]{:S(2)}) async-start(), calls=%async_computation.5 | async-start | bytes 1081344 | tf_op jit(solution)/shard_map/all_gather | solution.py:107
  11.3 31.3 %collective-permute-start.1 = (bf16[512,1024]{1,0:T(8,128)(2,1)}, bf16[512,1024]{1,0:T(8,128)(2,1)S(1)}, u32[]{:S(2)}, u32[]{:S(2)}) collective-permute-start(bf16[512,1024]{1,0:T(8,128)(2,1)} %bitcast.115), channel_id=1, source_target_pairs={{0,1},{1,2},{2,3},{3,4},{4,5},{5,6},{6,7},{7,8},{8,9},{9,10},{10,1... | collective-permute-start | bytes 3145736 | tf_op jit(solution)/shard_map/ppermute | solution.py:15
  15.9 23.8 %collective-permute-start = (bf16[512,1024]{1,0:T(8,128)(2,1)}, bf16[512,1024]{1,0:T(8,128)(2,1)}, u32[]{:S(2)}, u32[]{:S(2)}) collective-permute-start(bf16[512,1024]{1,0:T(8,128)(2,1)} %bitcast.111), channel_id=1, source_target_pairs={{0,1},{1,2},{2,3},{3,4},{4,5},{5,6},{6,7},{7,8},{8,9},{9,10},{10,1... | collective-permute-start | bytes 3145736 | tf_op jit(solution)/shard_map/ppermute | solution.py:15
  20.4 694.8 %reduce-scatter.5.cloned.1.call-start = ((), (), s32[]{:S(2)}) async-start(), calls=%async_computation.3 | async-start | bytes 1081344 | tf_op jit(solution)/shard_map/reduce_scatter | solution.py:213
  29.7 10.0 %copy-start.4 = (bf16[1,512,1024]{2,1,0:T(8,128)(2,1)S(1)}, bf16[1,512,1024]{2,1,0:T(8,128)(2,1)}, u32[]{:S(2)}) copy-start(bf16[1,512,1024]{2,1,0:T(8,128)(2,1)} %param.19) | copy-start | bytes 3145732
  33.3 9.3 copy-start.5
  636.4 3.1 copy-start.3
  639.4 156.9 %reduce-scatter.3.cloned.1.call-start = ((), (), s32[]{:S(2)}) async-start(), calls=%async_computation.2 | async-start | bytes 1081344 | tf_op jit(solution)/shard_map/reduce_scatter | solution.py:210
  640.7 315.6 %all-reduce.2.cloned.1.call-start = ((), (), s32[]{:S(2)}) async-start(), calls=%async_computation.4 | async-start | bytes 8388608 | tf_op jit(solution)/shard_map/psum | solution.py:222
  642.5 16.1 %collective-permute-start.3 = (bf16[512,1024]{1,0:T(8,128)(2,1)S(1)}, bf16[512,1024]{1,0:T(8,128)(2,1)S(1)}, u32[]{:S(2)}, u32[]{:S(2)}) collective-permute-start(bf16[512,1024]{1,0:T(8,128)(2,1)S(1)} %slice.88), channel_id=1, source_target_pairs={{1,0},{2,1},{3,2},{4,3},{5,4},{6,5},{7,6},{8,7},{9,8},{10,9},{11,1... | collective-permute-start | bytes 3145736 | tf_op jit(solution)/shard_map/ppermute | solution.py:15
  649.6 20.2 %copy-start.2 = (f32[1024,1024]{1,0:T(8,128)S(1)}, f32[1024,1024]{1,0:T(8,128)}, u32[]{:S(2)}) copy-start(f32[1024,1024]{1,0:T(8,128)} %get-tuple-element.279) | copy-start | bytes 12582916
  651.6 18.3 %collective-permute-start.2 = (bf16[512,1024]{1,0:T(8,128)(2,1)S(1)}, bf16[512,1024]{1,0:T(8,128)(2,1)S(1)}, u32[]{:S(2)}, u32[]{:S(2)}) collective-permute-start(bf16[512,1024]{1,0:T(8,128)(2,1)S(1)} %slice.89), channel_id=1, source_target_pairs={{1,0},{2,1},{3,2},{4,3},{5,4},{6,5},{7,6},{8,7},{9,8},{10,9},{11,1... | collective-permute-start | bytes 3145736 | tf_op jit(solution)/shard_map/ppermute | solution.py:15
  801.3 160.0 %copy-start.1 = (bf16[1024,1024]{1,0:T(8,128)(2,1)S(1)}, bf16[1024,1024]{1,0:T(8,128)(2,1)}, u32[]{:S(2)}) copy-start(bf16[1024,1024]{1,0:T(8,128)(2,1)} %param.22) | copy-start | bytes 6291460
Sparse Core Ops, SparseCore 0:
  11.4 52.4 all-gather.6
  66.7 41.9 all-gather.4
  639.6 75.6 reduce-scatter.4
  719.5 76.7 reduce-scatter.2
  801.1 155.0 all-reduce.1
where the time goes:
time: 972 us; the launch traced here: 968 us
  matrix products  379 us (39%)
  waiting for transfers between devices  361 us (37%)
  local copies, waits for them, and re-layouts  166 us (17%)
  other arithmetic  35.4 us (4%)
  between operations  13.9 us (1%)
  starting transfers between devices  11.1 us (1%)
    psum x1, waiting for transfers between devices, per_device(): weight_total = lax.psum(weight_part, ('fam', 'ctx'))  152 us
    dot_general x8, matrix products, attend(): jnp.einsum('gqk,kge->qge', grad_score, key_blk, preferred_element_type=jn...  108 us
    dot_general x8, matrix products, attend(): jnp.einsum('gqk,qge->kge', grad_score, query_blk, preferred_element_type=...  105 us
    reduce_scatter x1, waiting for transfers between devices, per_device(): lax.psum_scatter(mem_kgrad.astype(jnp.bfloat16), 'ctx', scatter_dimension...  79.4 us
    sub x8, matrix products, attend(): expo = jnp.where(live, jnp.exp(shifted - row_max), 0.0)  56 us
    dynamic_slice x88, local copies, waits for them, and re-layouts, columns_of(): return lax.dynamic_slice_in_dim(array, column, span, 1)  50 us
    all_gather x1, waiting for transfers between devices, per_device(): lax.all_gather(key_loc[own_slots], 'ctx', axis=0, tiled=True)  44.9 us
    reduce_scatter x1, waiting for transfers between devices, per_device(): lax.psum_scatter(mem_vgrad.astype(jnp.bfloat16), 'ctx', scatter_dimension...  43.8 us
  transfers between devices with their start and end apart: 9, of which 8 were waited for; matrix products, arithmetic and copies ran while one was open for 4% of the time, Pallas kernels for 0%

commit v1 on v0

--- a/solution.py
+++ b/solution.py
@@ -7,6 +7,9 @@
 W = 512
 BLK = 128
 NEG_FILL = -1e30
+mix_the_regions = lambda axis_key, incoming_x, dev_axis: jax.lax.psum(
+    jax.lax.psum(incoming_x, axis_key), dev_axis
+)
 
 
 def passed_along(value, axis, steps):
@@ -219,7 +222,7 @@
     weight_part = lax.dot_general(
         attn_rows, grad_out, (((0,), (0,)), ((), ())), preferred_element_type=jnp.float32
     )
-    weight_total = lax.psum(weight_part, ("fam", "ctx"))
+    weight_total = mix_the_regions("fam", weight_part, "ctx")
     weight_grad = weight_total * (lax.axis_size("fam") * ctx_size * tokens) ** (-0.5)
     return (
         query_grad.astype(jnp.bfloat16)[None],

time: 972 us -> 1030 us (1.060)
  waiting for transfers between devices: 361 us -> 413 us
    psum x1 -> x2, waiting for transfers between devices: 152 us -> 191 us  [the longest x1 108 us: jax.lax.psum(jax.lax.psum(incoming_x, axis_key), dev_axis)]
    reduce_scatter x1, waiting for transfers between devices: 43.8 us -> 60.1 us  [per_device(): lax.psum_scatter(mem_vgrad.astype(jnp.bfloat16), 'ctx', scatter_dimension...]
  transfers between devices with their start and end apart: 9 -> 10, of which waited for: 8 -> 8; matrix products, arithmetic and copies ran while one was open for 4% -> 4% of each run, Pallas kernels for 0% -> 0%
where the time goes in v1:
time: 1030 us; the launch traced here: 1020 us
  waiting for transfers between devices  413 us (40%)
  matrix products  379 us (37%)
  local copies, waits for them, and re-layouts  167 us (16%)
  other arithmetic  35.1 us (3%)
  between operations  14.3 us (1%)
  starting transfers between devices  11.5 us (1%)
    dot_general x8, matrix products, attend(): jnp.einsum('gqk,kge->qge', grad_score, key_blk, preferred_element_type=jn...  108 us
    psum x1, waiting for transfers between devices, jax.lax.psum(jax.lax.psum(incoming_x, axis_key), dev_axis)  108 us
    dot_general x8, matrix products, attend(): jnp.einsum('gqk,qge->kge', grad_score, query_blk, preferred_element_type=...  105 us
    psum x1, waiting for transfers between devices, jax.lax.psum(incoming_x, axis_key)  82.7 us
    reduce_scatter x1, waiting for transfers between devices, per_device(): lax.psum_scatter(mem_kgrad.astype(jnp.bfloat16), 'ctx', scatter_dimension...  79 us
    reduce_scatter x1, waiting for transfers between devices, per_device(): lax.psum_scatter(mem_vgrad.astype(jnp.bfloat16), 'ctx', scatter_dimension...  60.1 us
    sub x8, matrix products, attend(): expo = jnp.where(live, jnp.exp(shifted - row_max), 0.0)  56 us
    dynamic_slice x88, local copies, waits for them, and re-layouts, columns_of(): return lax.dynamic_slice_in_dim(array, column, span, 1)  50 us
  transfers between devices with their start and end apart: 10, of which 8 were waited for; matrix products, arithmetic and copies ran while one was open for 4% of the time, Pallas kernels for 0%

profile of v1, /device:TPU:1, one launch (start us, length us, event | category | flops | bytes accessed | tf_op | source)
XLA Modules:
  0.0 1021.9 jit_solution(18279666372157138422)
XLA Ops:
  44.0 19.9 %all-gather.7.cloned.1.call-done = bf16[512,1024]{1,0:T(8,128)(2,1)} async-done(((bf16[16,1024]{1,0:T(8,128)(2,1)}), bf16[512,1024]{1,0:T(8,128)(2,1)}) %all-gather.7.cloned.1.call-update) | async-done | bytes 1048592 | tf_op jit(solution)/shard_map/all_gather | solution.py:111
  63.9 44.9 %all-gather.5.cloned.1.call-done = bf16[512,1024]{1,0:T(8,128)(2,1)} async-done(((bf16[16,1024]{1,0:T(8,128)(2,1)}), bf16[512,1024]{1,0:T(8,128)(2,1)}) %all-gather.5.cloned.1.call-update) | async-done | bytes 1048592 | tf_op jit(solution)/shard_map/all_gather | solution.py:110
  118.0 518.4 %while.27 = (s32[]{:T(128)}, bf16[512,1024]{1,0:T(8,128)(2,1)}, f32[1024,1024]{1,0:T(8,128)}, f32[1024,1024]{1,0:T(8,128)}, f32[512,1024]{1,0:T(8,128)}, /*index...) while((s32[]{:T(128)}, bf16[512,1024]{1,0:T(8,128)(2,1)}, ...), condition=%wide.region_14.15_spmd, body=%wide.region_10.14_spmd.sunk | while | flops 1247747584 | bytes 80244984 | solution.py:203
  144.4 13.6 %fusion.101 = bf16[2,64,512]{2,1,0:T(8,128)(2,1)S(1)} fusion(f32[2,512,1536]{2,1,0:T(8,128)} %fusion.99, bf16[512,2,64]{0,2,1:T(8,128)(2,1)S(1)} %bitcast.109, bf16[1024,2,64]{0,2,1:T(8,128)(2,1)S(1)} %bitcast.104, f32[2,512,1536]{2,1,0:T(8,128)} %get-tuple-element.467, f32[2,512]{1,0:T(2,128)S(1)} %broadcast_maximum_fusion.2), kind=kOutput, calls=%fused_computation.16.clone.1 | convolution fusion | flops 213125632 | bytes 13111296 | tf_op jit(solution)/shard_map/while/body/eval_jaxpr/gqk,kge->qge/dot_general | solution.py:78
  157.9 13.2 %fusion.102 = f32[1536,2,64]{0,2,1:T(8,128)S(1)} fusion(bf16[512,2,64]{0,2,1:T(8,128)(2,1)S(1)} %bitcast.107, f32[2,512,1536]{2,1,0:T(8,128)} %fusion.99, f32[2,512,1536]{2,1,0:T(8,128)} %get-tuple-element.467, f32[2,512]{1,0:T(2,128)S(1)} %broadcast_maximum_fusion.2), kind=kOutput, calls=%fused_computation.18.clone.1 | convolution fusion | flops 212339200 | bytes 13504512 | tf_op jit(solution)/shard_map/while/body/eval_jaxpr/gqk,qge->kge/dot_general | solution.py:79
  209.2 13.6 %fusion.101 = bf16[2,64,512]{2,1,0:T(8,128)(2,1)S(1)} fusion(f32[2,512,1536]{2,1,0:T(8,128)} %fusion.99, bf16[512,2,64]{0,2,1:T(8,128)(2,1)S(1)} %bitcast.109, bf16[1024,2,64]{0,2,1:T(8,128)(2,1)S(1)} %bitcast.104, f32[2,512,1536]{2,1,0:T(8,128)} %get-tuple-element.467, f32[2,512]{1,0:T(2,128)S(1)} %broadcast_maximum_fusion.2), kind=kOutput, calls=%fused_computation.16.clone.1 | convolution fusion | flops 213125632 | bytes 13111296 | tf_op jit(solution)/shard_map/while/body/eval_jaxpr/gqk,kge->qge/dot_general | solution.py:78
  222.7 13.2 %fusion.102 = f32[1536,2,64]{0,2,1:T(8,128)S(1)} fusion(bf16[512,2,64]{0,2,1:T(8,128)(2,1)S(1)} %bitcast.107, f32[2,512,1536]{2,1,0:T(8,128)} %fusion.99, f32[2,512,1536]{2,1,0:T(8,128)} %get-tuple-element.467, f32[2,512]{1,0:T(2,128)S(1)} %broadcast_maximum_fusion.2), kind=kOutput, calls=%fused_computation.18.clone.1 | convolution fusion | flops 212339200 | bytes 13504512 | tf_op jit(solution)/shard_map/while/body/eval_jaxpr/gqk,qge->kge/dot_general | solution.py:79
  274.0 13.6 %fusion.101 = bf16[2,64,512]{2,1,0:T(8,128)(2,1)S(1)} fusion(f32[2,512,1536]{2,1,0:T(8,128)} %fusion.99, bf16[512,2,64]{0,2,1:T(8,128)(2,1)S(1)} %bitcast.109, bf16[1024,2,64]{0,2,1:T(8,128)(2,1)S(1)} %bitcast.104, f32[2,512,1536]{2,1,0:T(8,128)} %get-tuple-element.467, f32[2,512]{1,0:T(2,128)S(1)} %broadcast_maximum_fusion.2), kind=kOutput, calls=%fused_computation.16.clone.1 | convolution fusion | flops 213125632 | bytes 13111296 | tf_op jit(solution)/shard_map/while/body/eval_jaxpr/gqk,kge->qge/dot_general | solution.py:78
  287.5 13.2 %fusion.102 = f32[1536,2,64]{0,2,1:T(8,128)S(1)} fusion(bf16[512,2,64]{0,2,1:T(8,128)(2,1)S(1)} %bitcast.107, f32[2,512,1536]{2,1,0:T(8,128)} %fusion.99, f32[2,512,1536]{2,1,0:T(8,128)} %get-tuple-element.467, f32[2,512]{1,0:T(2,128)S(1)} %broadcast_maximum_fusion.2), kind=kOutput, calls=%fused_computation.18.clone.1 | convolution fusion | flops 212339200 | bytes 13504512 | tf_op jit(solution)/shard_map/while/body/eval_jaxpr/gqk,qge->kge/dot_general | solution.py:79
  338.8 13.6 %fusion.101 = bf16[2,64,512]{2,1,0:T(8,128)(2,1)S(1)} fusion(f32[2,512,1536]{2,1,0:T(8,128)} %fusion.99, bf16[512,2,64]{0,2,1:T(8,128)(2,1)S(1)} %bitcast.109, bf16[1024,2,64]{0,2,1:T(8,128)(2,1)S(1)} %bitcast.104, f32[2,512,1536]{2,1,0:T(8,128)} %get-tuple-element.467, f32[2,512]{1,0:T(2,128)S(1)} %broadcast_maximum_fusion.2), kind=kOutput, calls=%fused_computation.16.clone.1 | convolution fusion | flops 213125632 | bytes 13111296 | tf_op jit(solution)/shard_map/while/body/eval_jaxpr/gqk,kge->qge/dot_general | solution.py:78
  352.4 13.2 %fusion.102 = f32[1536,2,64]{0,2,1:T(8,128)S(1)} fusion(bf16[512,2,64]{0,2,1:T(8,128)(2,1)S(1)} %bitcast.107, f32[2,512,1536]{2,1,0:T(8,128)} %fusion.99, f32[2,512,1536]{2,1,0:T(8,128)} %get-tuple-element.467, f32[2,512]{1,0:T(2,128)S(1)} %broadcast_maximum_fusion.2), kind=kOutput, calls=%fused_computation.18.clone.1 | convolution fusion | flops 212339200 | bytes 13504512 | tf_op jit(solution)/shard_map/while/body/eval_jaxpr/gqk,qge->kge/dot_general | solution.py:79
  403.6 13.6 %fusion.101 = bf16[2,64,512]{2,1,0:T(8,128)(2,1)S(1)} fusion(f32[2,512,1536]{2,1,0:T(8,128)} %fusion.99, bf16[512,2,64]{0,2,1:T(8,128)(2,1)S(1)} %bitcast.109, bf16[1024,2,64]{0,2,1:T(8,128)(2,1)S(1)} %bitcast.104, f32[2,512,1536]{2,1,0:T(8,128)} %get-tuple-element.467, f32[2,512]{1,0:T(2,128)S(1)} %broadcast_maximum_fusion.2), kind=kOutput, calls=%fused_computation.16.clone.1 | convolution fusion | flops 213125632 | bytes 13111296 | tf_op jit(solution)/shard_map/while/body/eval_jaxpr/gqk,kge->qge/dot_general | solution.py:78
  417.2 13.2 %fusion.102 = f32[1536,2,64]{0,2,1:T(8,128)S(1)} fusion(bf16[512,2,64]{0,2,1:T(8,128)(2,1)S(1)} %bitcast.107, f32[2,512,1536]{2,1,0:T(8,128)} %fusion.99, f32[2,512,1536]{2,1,0:T(8,128)} %get-tuple-element.467, f32[2,512]{1,0:T(2,128)S(1)} %broadcast_maximum_fusion.2), kind=kOutput, calls=%fused_computation.18.clone.1 | convolution fusion | flops 212339200 | bytes 13504512 | tf_op jit(solution)/shard_map/while/body/eval_jaxpr/gqk,qge->kge/dot_general | solution.py:79
  468.4 13.6 %fusion.101 = bf16[2,64,512]{2,1,0:T(8,128)(2,1)S(1)} fusion(f32[2,512,1536]{2,1,0:T(8,128)} %fusion.99, bf16[512,2,64]{0,2,1:T(8,128)(2,1)S(1)} %bitcast.109, bf16[1024,2,64]{0,2,1:T(8,128)(2,1)S(1)} %bitcast.104, f32[2,512,1536]{2,1,0:T(8,128)} %get-tuple-element.467, f32[2,512]{1,0:T(2,128)S(1)} %broadcast_maximum_fusion.2), kind=kOutput, calls=%fused_computation.16.clone.1 | convolution fusion | flops 213125632 | bytes 13111296 | tf_op jit(solution)/shard_map/while/body/eval_jaxpr/gqk,kge->qge/dot_general | solution.py:78
  482.0 13.2 %fusion.102 = f32[1536,2,64]{0,2,1:T(8,128)S(1)} fusion(bf16[512,2,64]{0,2,1:T(8,128)(2,1)S(1)} %bitcast.107, f32[2,512,1536]{2,1,0:T(8,128)} %fusion.99, f32[2,512,1536]{2,1,0:T(8,128)} %get-tuple-element.467, f32[2,512]{1,0:T(2,128)S(1)} %broadcast_maximum_fusion.2), kind=kOutput, calls=%fused_computation.18.clone.1 | convolution fusion | flops 212339200 | bytes 13504512 | tf_op jit(solution)/shard_map/while/body/eval_jaxpr/gqk,qge->kge/dot_general | solution.py:79
  533.2 13.6 %fusion.101 = bf16[2,64,512]{2,1,0:T(8,128)(2,1)S(1)} fusion(f32[2,512,1536]{2,1,0:T(8,128)} %fusion.99, bf16[512,2,64]{0,2,1:T(8,128)(2,1)S(1)} %bitcast.109, bf16[1024,2,64]{0,2,1:T(8,128)(2,1)S(1)} %bitcast.104, f32[2,512,1536]{2,1,0:T(8,128)} %get-tuple-element.467, f32[2,512]{1,0:T(2,128)S(1)} %broadcast_maximum_fusion.2), kind=kOutput, calls=%fused_computation.16.clone.1 | convolution fusion | flops 213125632 | bytes 13111296 | tf_op jit(solution)/shard_map/while/body/eval_jaxpr/gqk,kge->qge/dot_general | solution.py:78
  546.8 13.2 %fusion.102 = f32[1536,2,64]{0,2,1:T(8,128)S(1)} fusion(bf16[512,2,64]{0,2,1:T(8,128)(2,1)S(1)} %bitcast.107, f32[2,512,1536]{2,1,0:T(8,128)} %fusion.99, f32[2,512,1536]{2,1,0:T(8,128)} %get-tuple-element.467, f32[2,512]{1,0:T(2,128)S(1)} %broadcast_maximum_fusion.2), kind=kOutput, calls=%fused_computation.18.clone.1 | convolution fusion | flops 212339200 | bytes 13504512 | tf_op jit(solution)/shard_map/while/body/eval_jaxpr/gqk,qge->kge/dot_general | solution.py:79
  598.0 13.6 %fusion.101 = bf16[2,64,512]{2,1,0:T(8,128)(2,1)S(1)} fusion(f32[2,512,1536]{2,1,0:T(8,128)} %fusion.99, bf16[512,2,64]{0,2,1:T(8,128)(2,1)S(1)} %bitcast.109, bf16[1024,2,64]{0,2,1:T(8,128)(2,1)S(1)} %bitcast.104, f32[2,512,1536]{2,1,0:T(8,128)} %get-tuple-element.467, f32[2,512]{1,0:T(2,128)S(1)} %broadcast_maximum_fusion.2), kind=kOutput, calls=%fused_computation.16.clone.1 | convolution fusion | flops 213125632 | bytes 13111296 | tf_op jit(solution)/shard_map/while/body/eval_jaxpr/gqk,kge->qge/dot_general | solution.py:78
  611.6 13.2 %fusion.102 = f32[1536,2,64]{0,2,1:T(8,128)S(1)} fusion(bf16[512,2,64]{0,2,1:T(8,128)(2,1)S(1)} %bitcast.107, f32[2,512,1536]{2,1,0:T(8,128)} %fusion.99, f32[2,512,1536]{2,1,0:T(8,128)} %get-tuple-element.467, f32[2,512]{1,0:T(2,128)S(1)} %broadcast_maximum_fusion.2), kind=kOutput, calls=%fused_computation.18.clone.1 | convolution fusion | flops 212339200 | bytes 13504512 | tf_op jit(solution)/shard_map/while/body/eval_jaxpr/gqk,qge->kge/dot_general | solution.py:79
  650.7 82.7 %all-reduce.3.cloned.1.call-done = f32[1024,1024]{1,0:T(8,128)} async-done(((f32[1024,1024]{1,0:T(8,128)}), f32[1024,1024]{1,0:T(8,128)}) %all-reduce.3.cloned.1.call-update) | async-done | bytes 4194320 | tf_op jit(solution)/shard_map/psum | solution.py:11
  740.0 11.5 %collective-permute-done.2 = bf16[512,1024]{1,0:T(8,128)(2,1)S(1)} collective-permute-done((bf16[512,1024]{1,0:T(8,128)(2,1)S(1)}, bf16[512,1024]{1,0:T(8,128)(2,1)S(1)}, u32[]{:S(2)}, u32[]{:S(2)}) %collective-permute-start.2) | collective-permute-done | bytes 1048608 | tf_op jit(solution)/shard_map/ppermute | solution.py:18
  753.1 60.1 %reduce-scatter.5.cloned.1.call-done = bf16[16,1024]{1,0:T(8,128)(2,1)} async-done(((bf16[512,1024]{1,0:T(8,128)(2,1)}), bf16[16,1024]{1,0:T(8,128)(2,1)}) %reduce-scatter.5.cloned.1.call-update) | async-done | bytes 32784 | tf_op jit(solution)/shard_map/reduce_scatter | solution.py:216
  815.0 79.0 %reduce-scatter.3.cloned.1.call-done = bf16[16,1024]{1,0:T(8,128)(2,1)} async-done(((bf16[512,1024]{1,0:T(8,128)(2,1)}), bf16[16,1024]{1,0:T(8,128)(2,1)}) %reduce-scatter.3.cloned.1.call-update) | async-done | bytes 32784 | tf_op jit(solution)/shard_map/reduce_scatter | solution.py:213
  901.8 108.2 %all-reduce.5.cloned.1.call-done = f32[1024,1024]{1,0:T(8,128)} async-done(((f32[1024,1024]{1,0:T(8,128)}), f32[1024,1024]{1,0:T(8,128)}) %all-reduce.5.cloned.1.call-update) | async-done | bytes 4194320 | tf_op jit(solution)/shard_map/psum | solution.py:10
  (406 shorter events, 386.0 us)
Async XLA Ops:
  7.2 22.5 %copy-start = (bf16[1024,1024]{1,0:T(8,128)(2,1)S(1)}, bf16[1024,1024]{1,0:T(8,128)(2,1)}, u32[]{:S(2)}) copy-start(bf16[1024,1024]{1,0:T(8,128)(2,1)} %param.22) | copy-start | bytes 6291460
  7.2 56.7 %all-gather.7.cloned.1.call-start = ((), (), s32[]{:S(2)}) async-start(), calls=%async_computation.7 | async-start | bytes 1081344 | tf_op jit(solution)/shard_map/all_gather | solution.py:111
  8.1 0.5 copy-start.6
  11.2 97.5 %all-gather.5.cloned.1.call-start = ((), (), s32[]{:S(2)}) async-start(), calls=%async_computation.6 | async-start | bytes 1081344 | tf_op jit(solution)/shard_map/all_gather | solution.py:110
  11.3 31.3 %collective-permute-start.1 = (bf16[512,1024]{1,0:T(8,128)(2,1)}, bf16[512,1024]{1,0:T(8,128)(2,1)S(1)}, u32[]{:S(2)}, u32[]{:S(2)}) collective-permute-start(bf16[512,1024]{1,0:T(8,128)(2,1)} %bitcast.115), channel_id=1, source_target_pairs={{0,1},{1,2},{2,3},{3,4},{4,5},{5,6},{6,7},{7,8},{8,9},{9,10},{10,1... | collective-permute-start | bytes 3145736 | tf_op jit(solution)/shard_map/ppermute | solution.py:18
  15.9 23.8 %collective-permute-start = (bf16[512,1024]{1,0:T(8,128)(2,1)}, bf16[512,1024]{1,0:T(8,128)(2,1)}, u32[]{:S(2)}, u32[]{:S(2)}) collective-permute-start(bf16[512,1024]{1,0:T(8,128)(2,1)} %bitcast.111), channel_id=1, source_target_pairs={{0,1},{1,2},{2,3},{3,4},{4,5},{5,6},{6,7},{7,8},{8,9},{9,10},{10,1... | collective-permute-start | bytes 3145736 | tf_op jit(solution)/shard_map/ppermute | solution.py:18
  20.4 713.0 %all-reduce.3.cloned.1.call-start = ((), (), s32[]{:S(2)}) async-start(), calls=%async_computation.4 | async-start | bytes 8388608 | tf_op jit(solution)/shard_map/psum | solution.py:11
  29.7 10.0 copy-start.4
  33.3 9.3 copy-start.5
  641.2 1.6 copy-start.3
  641.2 172.0 %reduce-scatter.5.cloned.1.call-start = ((), (), s32[]{:S(2)}) async-start(), calls=%async_computation.3 | async-start | bytes 1081344 | tf_op jit(solution)/shard_map/reduce_scatter | solution.py:216
  644.0 250.0 %reduce-scatter.3.cloned.1.call-start = ((), (), s32[]{:S(2)}) async-start(), calls=%async_computation.2 | async-start | bytes 1081344 | tf_op jit(solution)/shard_map/reduce_scatter | solution.py:213
  646.8 363.3 %all-reduce.5.cloned.1.call-start = ((), (), s32[]{:S(2)}) async-start(), calls=%async_computation.5 | async-start | bytes 8388608 | tf_op jit(solution)/shard_map/psum | solution.py:10
  648.6 89.4 %collective-permute-start.3 = (bf16[512,1024]{1,0:T(8,128)(2,1)S(1)}, bf16[512,1024]{1,0:T(8,128)(2,1)S(1)}, u32[]{:S(2)}, u32[]{:S(2)}) collective-permute-start(bf16[512,1024]{1,0:T(8,128)(2,1)S(1)} %slice.88), channel_id=1, source_target_pairs={{1,0},{2,1},{3,2},{4,3},{5,4},{6,5},{7,6},{8,7},{9,8},{10,9},{11,1... | collective-permute-start | bytes 3145736 | tf_op jit(solution)/shard_map/ppermute | solution.py:18
  733.4 18.1 %copy-start.2 = (f32[1024,1024]{1,0:T(8,128)S(1)}, f32[1024,1024]{1,0:T(8,128)}, u32[]{:S(2)}) copy-start(f32[1024,1024]{1,0:T(8,128)} %get-tuple-element.279) | copy-start | bytes 12582916
  735.3 16.1 %collective-permute-start.2 = (bf16[512,1024]{1,0:T(8,128)(2,1)S(1)}, bf16[512,1024]{1,0:T(8,128)(2,1)S(1)}, u32[]{:S(2)}, u32[]{:S(2)}) collective-permute-start(bf16[512,1024]{1,0:T(8,128)(2,1)S(1)} %slice.89), channel_id=1, source_target_pairs={{1,0},{2,1},{3,2},{4,3},{5,4},{6,5},{7,6},{8,7},{9,8},{10,9},{11,1... | collective-permute-start | bytes 3145736 | tf_op jit(solution)/shard_map/ppermute | solution.py:18
  898.9 116.2 %copy-start.1 = (bf16[1024,1024]{1,0:T(8,128)(2,1)S(1)}, bf16[1024,1024]{1,0:T(8,128)(2,1)}, u32[]{:S(2)}) copy-start(bf16[1024,1024]{1,0:T(8,128)(2,1)} %param.22) | copy-start | bytes 6291460
Sparse Core Ops, SparseCore 0:
  11.4 52.4 all-gather.6
  66.7 41.9 all-gather.4
  641.3 92.0 all-reduce.2
  737.7 75.4 reduce-scatter.4
  817.2 76.7 reduce-scatter.2
  897.5 112.4 all-reduce.4
